TPU v7x, 256 devices: a whole 4x4x8 slice. The times are simulated.
256 devices in a mesh: sta: 64 (over y, x, z_hi, core), win: 4 (over z_lo).
Axes of the slice: x: 4, y: 4, z: 8 (z_hi: 2, z_lo: 4; z = z_hi * 4 + z_lo), core: 2. Of those that a mesh axis runs over, the one named last changes fastest.
Arguments:
- records: bfloat16 [16, 4096, 2048], P('win', 'sta'), may hold values from -6 to 6
- record_block: int32 [16, 4096, 1], P('win', 'sta'), may hold values from 0 to 63; in each aligned block of 64 rows (0 to 63, 64 to 127, ..., all dimensions but the last counted through in order) at most 2 rows name the same one
- record_station: int32 [16, 4096], P('win', 'sta'), may hold values from 0 to 31
- quality: int32 [16, 4096], P('win', 'sta'), may hold values 0 or 1
Outputs:
- correlation: bfloat16 [2, 32, 2048, 2048], P(None, 'win', 'sta')
Inputs may be any that keep to these rules, and one draw needn't show every extreme that they name: `record_block`: in each hour, of the 64 records that one index of sta holds, at most 2 name one station block, and some block is named by exactly 2 of them.
All inputs are finite; a program needn't handle non-finite values. No bound on the sum of `quality` on one device may be relied on, other than what follows from the above.
Results may differ from a plain program's by a relative error of at most 0.0071.
Values may be sent and summed in bfloat16 or wider, within the bound.
A program may use at most 128 MiB of HBM per device.

v0:
```python
import math

import jax
import jax.numpy as jnp
import numpy as np
from jax import lax
from jax.experimental import pallas as pl
from jax.experimental.pallas import tpu as pltpu
from jax.sharding import PartitionSpec as P

MESH = pl.DeviceIdType.MESH
BINS = 1024
LAGS = 2048
SMOOTH = 32
ROUNDS = 2
EPSILON = 1e-05
HOURS_DEV = 4
RECS_DEV = 64
WIN = 4
STA = 64
PLANE = 32
PIECES = 4
PB = BINS // PIECES
PW = 2 * PB
LANES = 128

OFFSETS = sorted(
    [(dy, dx, dc) for dy in range(4) for dx in range(4) for dc in range(2)][1:],
    key=lambda t: min(t[0], 4 - t[0]) + min(t[1], 4 - t[1]),
)


def remote(src, dst, send, recv, device):
    return pltpu.make_async_remote_copy(
        src_ref=src, dst_ref=dst, send_sem=send, recv_sem=recv, device_id=device, device_id_type=MESH
    )


def kernel(
    rows, key_col, rec, cos_u, sin_u, cos_v, sin_v, out,
    sbuf, rbuf, tag_s, tag_r, assign, psum, zsend, zrecv, mag_hi, mag_lo, gath, part, part32, table, stack, acc,
    plane_send, plane_recv, tag_send, tag_recv, z_send, z_recv, g_send, g_recv, p_send, p_recv,
):
    sta, win = lax.axis_index("sta"), lax.axis_index("win")
    y, x, zh, core = sta // 16, (sta // 4) % 4, (sta // 2) % 2, sta % 2
    slot = (sta // 4) * 2 + core

    def plane_peer(offset):
        y2, x2, c2 = (y + offset[0]) % 4, (x + offset[1]) % 4, (core + offset[2]) % 2
        return (((y2 * 4 + x2) * 2 + zh) * 2 + c2, win), (y2 * 4 + x2) * 2 + c2

    z_peer = (sta + 2 - 4 * zh, win)
    win_peers = [(sta, (win + d) % WIN) for d in range(1, WIN)]

    barrier = pltpu.get_barrier_semaphore()
    greeted = [plane_peer(o)[0] for o in OFFSETS] + [z_peer] + win_peers
    greeted += [((sta + d) % STA, w2) for d in (1, 2, STA - 1, STA - 2) for w2 in range(WIN)]
    for device in greeted:
        pl.semaphore_signal(barrier, inc=1, device_id=device, device_id_type=MESH)

    count = HOURS_DEV * RECS_DEV
    hour_row = lax.broadcasted_iota(jnp.int32, (1, count), 1) // RECS_DEV
    hour_col = lax.broadcasted_iota(jnp.int32, (count, 1), 0) // RECS_DEV
    block = rows[0:1, :]
    key_r = block + hour_row * STA
    key_c = key_col[...] + hour_col * STA
    before = lax.broadcasted_iota(jnp.int32, (count, count), 0) < lax.broadcasted_iota(jnp.int32, (count, count), 1)
    rank = jnp.sum(jnp.where(before & (key_c == key_r), 1.0, 0.0), axis=0, keepdims=True).astype(jnp.int32)
    target = ((block // 4) * 2 + block % 2) * 16 + hour_row * 4 + ((block // 2) % 2) * 2 + rank
    target = jnp.where(rows[2:3, :] > 0, target, -1)
    chosen = lax.broadcasted_iota(jnp.int32, (PLANE * 16, count), 0) == target
    tags = jnp.sum(jnp.where(chosen, (rows[1:2, :] + 1).astype(jnp.float32), 0.0), axis=1, keepdims=True)
    tag_s[...] = jnp.broadcast_to(tags, (PLANE * 16, LANES)).astype(jnp.bfloat16).reshape(PLANE, 16, LANES)
    placing = jnp.where(chosen, 1.0, 0.0).astype(jnp.bfloat16)

    pl.semaphore_wait(barrier, len(greeted))

    for offset in OFFSETS:
        device, place = plane_peer(offset)
        remote(tag_s.at[place], tag_r.at[slot], tag_send, tag_recv, device).start()
    tag_r[slot] = tag_s[slot]
    for p in range(PIECES):
        for half in range(2):
            lanes = pl.ds(half * BINS + p * PB, PB)
            packed = jnp.dot(placing, rec[:, lanes], preferred_element_type=jnp.float32)
            sbuf[p, :, :, half * PB : (half + 1) * PB] = packed.astype(jnp.bfloat16).reshape(PLANE, 16, PB)
        for offset in OFFSETS:
            device, place = plane_peer(offset)
            remote(sbuf.at[p, place], rbuf.at[p, slot], plane_send.at[p], plane_recv.at[p], device).start()
        rbuf[p, slot] = sbuf[p, slot]

    for p in range(PIECES):

        @pl.loop(0, PB // 32)
        def _(i, p=p):
            u = p * (PB // 32) + i
            row = pl.multiple_of(i * 32, 32)
            for n in range(LAGS // 512):
                lanes = pl.ds(n * 512, 512)
                cu, su = cos_u[pl.ds(u, 1), lanes], sin_u[pl.ds(u, 1), lanes]
                cv, sv = cos_v[:, lanes], sin_v[:, lanes]
                table[p, pl.ds(row, 32), lanes] = (cu * cv - su * sv).astype(jnp.bfloat16)
                table[p, pl.ds(PB + row, 32), lanes] = (-(su * cv) - cu * sv).astype(jnp.bfloat16)

    spare = PLANE - 1
    remote(tag_s.at[pl.ds(0, spare)], tag_r.at[pl.ds(0, spare)], tag_send, tag_recv, z_peer).wait_recv()
    arrived = tag_r[...].astype(jnp.float32).astype(jnp.int32).reshape(PLANE * 16, LANES) - 1
    row_id = lax.broadcasted_iota(jnp.int32, (PLANE * 16, LANES), 0)
    member = ((row_id // 2 + zh) % 2) * 128 + (arrived // 8) * 32 + ((row_id // 4) % 4) * 8 + arrived % 8
    member = jnp.where(arrived >= 0, member, -1)
    lane_id = lax.broadcasted_iota(jnp.int32, (PLANE * 16, LANES), 1)
    for half in range(2):
        hit = jnp.where(member == lane_id + half * LANES, 1.0, 0.0)
        assign[half * LANES : (half + 1) * LANES, :] = hit.T.astype(jnp.bfloat16)
    for p in range(PIECES):
        remote(
            sbuf.at[p, pl.ds(0, spare)], rbuf.at[p, pl.ds(0, spare)], plane_send.at[p], plane_recv.at[p], z_peer
        ).wait_recv()
        sums = jnp.dot(assign[...], rbuf[p].reshape(PLANE * 16, PW), preferred_element_type=jnp.float32)
        psum[p] = sums[:128]
        zsend[p] = sums[128:].astype(jnp.bfloat16)
        remote(zsend.at[p], zrecv.at[p], z_send.at[p], z_recv.at[p], z_peer).start()

    def magnitude(p):
        remote(zsend.at[p], zrecv.at[p], z_send.at[p], z_recv.at[p], z_peer).wait_recv()
        summed = psum[p] + zrecv[p].astype(jnp.float32)
        psum[p] = summed
        re, im = summed[:, :PB], summed[:, PB:]
        mag = jnp.sqrt(re * re + im * im)
        high = mag.astype(jnp.bfloat16)
        mag_hi[p] = high
        mag_lo[p] = (mag - high.astype(jnp.float32)).astype(jnp.bfloat16)

    band_k = lax.broadcasted_iota(jnp.int32, (PW, PB), 0) - LANES
    band_n = lax.broadcasted_iota(jnp.int32, (PW, PB), 1)
    band = jnp.where(jnp.abs(band_k - band_n) <= SMOOTH, 1.0, 0.0).astype(jnp.bfloat16)

    def whiten(p):
        last, following = (p - 1) % PIECES, (p + 1) % PIECES
        level = jnp.zeros((128, PB), jnp.float32)
        for mag in (mag_hi, mag_lo):
            around = jnp.concatenate([mag[last, :, PB - LANES :], mag[p], mag[following, :, :LANES]], axis=1)
            level += jnp.dot(around, band, preferred_element_type=jnp.float32)
        inverse = 1.0 / (level * (1.0 / (2 * SMOOTH + 1)) + EPSILON)
        gath[p, win] = (psum[p] * jnp.concatenate([inverse, inverse], axis=1)).astype(jnp.bfloat16)
        mine = gath.at[p, win]
        for device in win_peers:
            remote(mine, mine, g_send.at[p], g_recv.at[p], device).start()
        for r in range(ROUNDS):
            for w2 in range(WIN):
                remote(
                    gath.at[p, win, pl.ds(w2 * 32, 32)], part.at[p, r, win], p_send.at[p], p_recv.at[p],
                    ((sta + r + 1) % STA, w2),
                ).start()

    magnitude(0)
    magnitude(1)
    for p in (1, 2):
        magnitude(p + 1)
        whiten(p)
    whiten(3)
    whiten(0)

    def finish(p, first):
        remote(
            gath.at[p, pl.ds(0, WIN - 1)], gath.at[p, pl.ds(0, WIN - 1)], g_send.at[p], g_recv.at[p], z_peer
        ).wait_recv()
        remote(part.at[p], part.at[p], p_send.at[p], p_recv.at[p], z_peer).wait_recv()
        part32[...] = part[p].astype(jnp.float32)

        @pl.loop(0, PB // LANES)
        def _(t):
            re = pl.ds(pl.multiple_of(t * LANES, LANES), LANES)
            im = pl.ds(pl.multiple_of(PB + t * LANES, LANES), LANES)
            for g in range(4):
                r = g // 2
                sums = [[[jnp.zeros((8, LANES), jnp.float32) for _ in range(2)] for _ in range(4)] for _ in range(4)]
                for w2 in range(WIN):
                    for pair in range(2):
                        own = []
                        for octet in range(4):
                            at = pl.ds(octet * 32 + pair * 16, 16)
                            own.append(
                                (gath[p, w2, at, re].astype(jnp.float32), gath[p, w2, at, im].astype(jnp.float32))
                            )
                        for e in range(2):
                            for jj in range(4):
                                row = (pair * 2 + e) * 8 + (g % 2) * 4 + jj
                                pr = jnp.broadcast_to(part32[r, w2, row : row + 1, re], (8, LANES))
                                pi = jnp.broadcast_to(part32[r, w2, row : row + 1, im], (8, LANES))
                                for octet in range(4):
                                    a = own[octet][0][e * 8 : e * 8 + 8]
                                    c = own[octet][1][e * 8 : e * 8 + 8]
                                    both = sums[jj][octet]
                                    both[0] = both[0] + pr * a + pi * c
                                    both[1] = both[1] + pr * c - pi * a
                for jj in range(4):
                    at = pl.ds((r * 8 + (g % 2) * 4 + jj) * 32, 32)
                    for half, lanes in enumerate((re, im)):
                        tile = jnp.concatenate([sums[jj][octet][half] for octet in range(4)], axis=0)
                        stack[at, lanes] = tile.astype(jnp.bfloat16)

        @pl.loop(0, LAGS // 512)
        def _(n):
            lanes = pl.ds(pl.multiple_of(n * 512, 512), 512)
            more = jnp.dot(stack[...], table[p, :, lanes], preferred_element_type=jnp.float32)
            if first:
                acc[:, lanes] = more
            else:
                acc[:, lanes] += more

    finish(1, True)
    for p in (2, 3, 0):
        finish(p, False)
    out[...] = acc[...].astype(jnp.bfloat16).reshape(out.shape)

    remote(tag_s.at[pl.ds(0, spare)], tag_r.at[pl.ds(0, spare)], tag_send, tag_recv, z_peer).wait_send()
    for p in range(PIECES):
        remote(
            sbuf.at[p, pl.ds(0, spare)], rbuf.at[p, pl.ds(0, spare)], plane_send.at[p], plane_recv.at[p], z_peer
        ).wait_send()
        remote(zsend.at[p], zrecv.at[p], z_send.at[p], z_recv.at[p], z_peer).wait_send()
        remote(
            gath.at[p, pl.ds(0, WIN - 1)], gath.at[p, pl.ds(0, WIN - 1)], g_send.at[p], g_recv.at[p], z_peer
        ).wait_send()
        remote(part.at[p], part.at[p], p_send.at[p], p_recv.at[p], z_peer).wait_send()


def angles(multiples):
    turns = np.outer(multiples, np.arange(LAGS) - LAGS // 2) % (4 * BINS)
    return turns * (2.0 * math.pi / (4 * BINS))


def shards(records, record_block, record_station, quality):
    hours, count, wide = records.shape
    scaling = 1.0 / math.sqrt(2.0 * BINS * hours * WIN)
    coarse, fine = angles(np.arange(BINS // 32) * 32 + 1), angles(np.arange(32))
    cos_u, sin_u = jnp.asarray(np.cos(coarse) * scaling, jnp.float32), jnp.asarray(np.sin(coarse) * scaling, jnp.float32)
    cos_v, sin_v = jnp.asarray(np.cos(fine), jnp.float32), jnp.asarray(np.sin(fine), jnp.float32)
    rows = jnp.stack([a.reshape(hours * count) for a in (record_block, record_station, quality)])
    vmem = pl.BlockSpec(memory_space=pltpu.VMEM)
    dma = pltpu.SemaphoreType.DMA
    bf16, f32 = jnp.bfloat16, jnp.float32
    return pl.pallas_call(
        kernel,
        out_shape=jax.ShapeDtypeStruct((ROUNDS, 8, 32, LAGS), bf16),
        in_specs=[vmem] * 7,
        out_specs=vmem,
        scratch_shapes=[
            pltpu.VMEM((PIECES, PLANE, 16, PW), bf16),
            pltpu.VMEM((PIECES, PLANE, 16, PW), bf16),
            pltpu.VMEM((PLANE, 16, LANES), bf16),
            pltpu.VMEM((PLANE, 16, LANES), bf16),
            pltpu.VMEM((256, PLANE * 16), bf16),
            pltpu.VMEM((PIECES, 128, PW), f32),
            pltpu.VMEM((PIECES, 128, PW), bf16),
            pltpu.VMEM((PIECES, 128, PW), bf16),
            pltpu.VMEM((PIECES, 128, PB), bf16),
            pltpu.VMEM((PIECES, 128, PB), bf16),
            pltpu.VMEM((PIECES, WIN, 128, PW), bf16),
            pltpu.VMEM((PIECES, ROUNDS, WIN, 32, PW), bf16),
            pltpu.VMEM((ROUNDS, WIN, 32, PW), f32),
            pltpu.VMEM((PIECES, PW, LAGS), bf16),
            pltpu.VMEM((512, PW), bf16),
            pltpu.VMEM((512, LAGS), f32),
            dma((PIECES,)), dma((PIECES,)), dma, dma, dma((PIECES,)), dma((PIECES,)),
            dma((PIECES,)), dma((PIECES,)), dma((PIECES,)), dma((PIECES,)),
        ],
        compiler_params=pltpu.CompilerParams(
            collective_id=0, has_side_effects=True, vmem_limit_bytes=56 * 2**20
        ),
        name="correlate",
    )(rows, record_block.reshape(hours * count, 1), records.reshape(hours * count, wide), cos_u, sin_u, cos_v, sin_v)


def solution(mesh):
    in_specs = (P("win", "sta", None), P("win", "sta", None), P("win", "sta"), P("win", "sta"))
    out_specs = P(None, "win", "sta", None)
    return jax.shard_map(shards, mesh=mesh, in_specs=in_specs, out_specs=out_specs, check_vma=False)
```

profile of v0, /device:TPU:1, one launch (start us, length us, event | category | flops | bytes accessed | tf_op | source)
XLA Modules:
  0.0 136.7 jit_solution(17923278377895284730)
XLA Ops:
  0.0 0.8 stack_reshape.10
  0.8 0.8 stack_reshape.11
  1.5 0.5 broadcast.5
  2.0 1.3 reduce.5
  3.4 0.1 stack_reshape.9
  3.5 0.6 pad_add_fusion.rows
  4.1 1.5 %reshape.8.key_col = s32[256,1]{1,0:T(8,128)} reshape(s32[4,64]{1,0:T(4,128)} %bitcast.4) | data formatting | bytes 2048 | tf_op jit(solution)/shard_map/reshape | solution.py:273
  5.5 128.0 %correlate.1 = bf16[2,8,32,2048]{3,2,1,0:T(8,128)(2,1)} custom-call(s32[3,256]{1,0:T(4,128)} %pad_add_fusion.rows, s32[256,1]{1,0:T(8,128)} %reshape.8.key_col, bf16[256,2048]{1,0:T(8,128)(2,1)} %bitcast.3, f32[32,2048]{1,0:T(8,128)} %constant.8.clone.cos_u, f32[32,2048]{1,0:T(8,128)} %constant.9.clone.sin_u, f32[32,2048]{1,0:T(8,128)} %constant.10.clone.cos_v, ...), custom_call_target="tpu_custom_call" | custom-call | tf_op jit(solution)/shard_map/correlate/pallas_call | solution.py:244
  133.6 3.2 %copy.11 = bf16[2,8,32,2048]{3,2,1,0:T(8,128)(2,1)} copy(bf16[2,8,32,2048]{3,2,1,0:T(8,128)(2,1)} %correlate.1) | data formatting | bytes 4194304
where the time goes:
time: 137 us
  Pallas kernels  128 us (93%)
  local copies, waits for them, and re-layouts  6.75 us (5%)
  other arithmetic  1.95 us (1%)
    pallas_call x1, Pallas kernels, shards(): pl.pallas_call(kernel, out_shape=jax.ShapeDtypeStruct((ROUNDS, 8, 32, LAG...  128 us
    unnamed x2, local copies, waits for them, and re-layouts  3.67 us

commit v1 on v0

v1 whole, which is shorter than its diff:
```python
import math

import jax
import jax.numpy as jnp
import numpy as np
from jax import lax
from jax.experimental import pallas as pl
from jax.experimental.pallas import tpu as pltpu
from jax.sharding import PartitionSpec as P

MESH = pl.DeviceIdType.MESH
BINS = 1024
LAGS = 2048
SMOOTH = 32
ROUNDS = 2
EPSILON = 1e-05
HOURS_DEV = 4
RECS_DEV = 64
WIN = 4
STA = 64
PLANE = 32
PIECES = 4
PB = BINS // PIECES
PW = 2 * PB
LANES = 128

def remote(src, dst, send, recv, device):
    return pltpu.make_async_remote_copy(
        src_ref=src, dst_ref=dst, send_sem=send, recv_sem=recv, device_id=device, device_id_type=MESH
    )


def kernel(
    blocks, stations, quality, rec, cos_u, sin_u, cos_v, sin_v, out,
    sbuf, xbuf, rbuf, tag_s, tag_x, tag_r, assign, psum, zsend, zrecv, mag_hi, mag_lo, gath, part, part32, table, stack, acc,
    a_send, a_recv, b_send, b_recv, t_send, t_recv, z_send, z_recv, g_send, g_recv, c_send, c_recv, x_send, x_recv,
):
    sta, win = lax.axis_index("sta"), lax.axis_index("win")
    y, x, zh, core = sta // 16, (sta // 4) % 4, (sta // 2) % 2, sta % 2

    def in_plane(y2, x2, c2):
        return (((y2 * 4 + x2) * 2 + zh) * 2 + c2, win)

    z_peer = (sta + 2 - 4 * zh, win)
    other_core = (sta + 1 - 2 * core, win)

    barrier = pltpu.get_barrier_semaphore()
    greeted = [z_peer, other_core] + [(sta, (win + d) % WIN) for d in range(1, WIN)]
    greeted += [in_plane((y + d) % 4, x, (core + dc) % 2) for d in range(1, 4) for dc in range(2)]
    greeted += [in_plane(y, (x + d) % 4, (core + dc) % 2) for d in range(1, 4) for dc in range(2)]
    greeted += [((sta + d) % STA, w2) for d in (2, STA - 2) for w2 in range(WIN)]
    for device in greeted:
        pl.semaphore_signal(barrier, inc=1, device_id=device, device_id_type=MESH)

    count = HOURS_DEV * RECS_DEV
    hour_row = lax.broadcasted_iota(jnp.int32, (1, count), 1) // RECS_DEV
    block = jnp.concatenate([blocks[h] for h in range(HOURS_DEV)], axis=1)
    station = jnp.concatenate([stations[h : h + 1, :] for h in range(HOURS_DEV)], axis=1)
    passed = jnp.concatenate([quality[h : h + 1, :] for h in range(HOURS_DEV)], axis=1)
    key = (block + hour_row * STA).astype(jnp.float32)
    from_row = lax.broadcasted_iota(jnp.int32, (count, count), 0)
    to_row = lax.broadcasted_iota(jnp.int32, (count, count), 1)
    key_col = jnp.sum(jnp.where(from_row == to_row, key, 0.0), axis=1, keepdims=True)
    earlier = (from_row < to_row) & (key_col == key)
    rank = jnp.sum(jnp.where(earlier, 1.0, 0.0), axis=0, keepdims=True).astype(jnp.int32)
    target = ((block // 4) * 2 + block % 2) * 16 + hour_row * 4 + ((block // 2) % 2) * 2 + rank
    target = jnp.where(passed > 0, target, -1)
    chosen = lax.broadcasted_iota(jnp.int32, (PLANE * 16, count), 0) == target
    tags = jnp.sum(jnp.where(chosen, (station + 1).astype(jnp.float32), 0.0), axis=1, keepdims=True)
    tag_s[...] = jnp.broadcast_to(tags, (PLANE * 16, LANES)).astype(jnp.bfloat16).reshape(tag_s.shape)
    placing = jnp.where(chosen, 1.0, 0.0).astype(jnp.bfloat16)

    pl.semaphore_wait(barrier, len(greeted))

    def spread(source, between, send, recv, x_first):
        for d in range(1, 4):
            if x_first:
                x2 = (x + d) % 4
                remote(source.at[:, x2], between.at[x], send, recv, in_plane(y, x2, core)).start()
            else:
                y2 = (y + d) % 4
                remote(source.at[y2], between.at[y], send, recv, in_plane(y2, x, core)).start()
        own = source.at[:, x] if x_first else source.at[y]
        pltpu.make_async_copy(own, between.at[x if x_first else y], recv).start()

    def deliver(between, arrived, recv, send_on, recv_on, x_first):
        pltpu.make_async_copy(between, between, recv).wait()
        for d in (1, 2, 3, 0):
            for dc in (1, 0):
                c2 = (core + dc) % 2
                if x_first:
                    y2 = (y + d) % 4
                    src, dst, device = between.at[:, y2, c2], arrived.at[y, :, core], in_plane(y2, x, c2)
                else:
                    x2 = (x + d) % 4
                    src, dst, device = between.at[:, x2, c2], arrived.at[:, x, core], in_plane(y, x2, c2)
                if d or dc:
                    remote(src, dst, send_on, recv_on, device).start()
                else:
                    pltpu.make_async_copy(src, dst, recv_on).start()

    spread(tag_s, tag_x, t_send.at[0], t_recv.at[0], True)
    for p in range(PIECES):
        for half in range(2):
            lanes = pl.ds(half * BINS + p * PB, PB)
            packed = jnp.dot(placing, rec[:, lanes], preferred_element_type=jnp.float32)
            sbuf[p, :, :, :, :, half * PB : (half + 1) * PB] = packed.astype(jnp.bfloat16).reshape(4, 4, 2, 16, PB)
        spread(sbuf.at[p], xbuf.at[p], a_send.at[p], a_recv.at[p], p % 2 == 0)
    deliver(tag_x, tag_r, t_recv.at[0], t_send.at[1], t_recv.at[1], True)

    def weigh(p):
        @pl.loop(0, PB // 32)
        def _(i):
            u = p * (PB // 32) + i
            row = pl.multiple_of(i * 32, 32)
            for n in range(LAGS // 512):
                lanes = pl.ds(n * 512, 512)
                cu, su = cos_u[pl.ds(u, 1), lanes], sin_u[pl.ds(u, 1), lanes]
                cv, sv = cos_v[:, lanes], sin_v[:, lanes]
                table[p, pl.ds(row, 32), lanes] = (cu * cv - su * sv).astype(jnp.bfloat16)
                table[p, pl.ds(PB + row, 32), lanes] = (-(su * cv) - cu * sv).astype(jnp.bfloat16)

    weigh(0)
    weigh(1)
    for p in range(PIECES):
        deliver(xbuf.at[p], rbuf.at[p], a_recv.at[p], b_send.at[p], b_recv.at[p], p % 2 == 0)
    weigh(2)
    weigh(3)

    pltpu.make_async_copy(tag_r, tag_r, t_recv.at[1]).wait()
    label = tag_r[...].astype(jnp.float32).astype(jnp.int32).reshape(PLANE * 16, LANES) - 1
    row_id = lax.broadcasted_iota(jnp.int32, (PLANE * 16, LANES), 0)
    member = ((row_id // 2 + zh) % 2) * 128 + (label // 8) * 32 + ((row_id // 4) % 4) * 8 + label % 8
    member = jnp.where(label >= 0, member, -1)
    lane_id = lax.broadcasted_iota(jnp.int32, (PLANE * 16, LANES), 1)
    for half in range(2):
        hit = jnp.where(member == lane_id + half * LANES, 1.0, 0.0)
        assign[half * LANES : (half + 1) * LANES, :] = hit.T.astype(jnp.bfloat16)
    for p in range(PIECES):
        pltpu.make_async_copy(rbuf.at[p], rbuf.at[p], b_recv.at[p]).wait()
        sums = jnp.dot(assign[...], rbuf[p].reshape(PLANE * 16, PW), preferred_element_type=jnp.float32)
        psum[p] = sums[:128]
        zsend[p] = sums[128:].astype(jnp.bfloat16)
        remote(zsend.at[p], zrecv.at[p], z_send.at[p], z_recv.at[p], z_peer).start()

    def magnitude(p):
        pltpu.make_async_copy(zrecv.at[p], zrecv.at[p], z_recv.at[p]).wait()
        summed = psum[p] + zrecv[p].astype(jnp.float32)
        psum[p] = summed
        re, im = summed[:, :PB], summed[:, PB:]
        mag = jnp.sqrt(re * re + im * im)
        high = mag.astype(jnp.bfloat16)
        mag_hi[p] = high
        mag_lo[p] = (mag - high.astype(jnp.float32)).astype(jnp.bfloat16)

    band_k = lax.broadcasted_iota(jnp.int32, (PW, PB), 0) - LANES
    band_n = lax.broadcasted_iota(jnp.int32, (PW, PB), 1)
    band = jnp.where(jnp.abs(band_k - band_n) <= SMOOTH, 1.0, 0.0).astype(jnp.bfloat16)

    def whiten(p):
        last, following = (p - 1) % PIECES, (p + 1) % PIECES
        level = jnp.zeros((128, PB), jnp.float32)
        for mag in (mag_hi, mag_lo):
            around = jnp.concatenate([mag[last, :, PB - LANES :], mag[p], mag[following, :, :LANES]], axis=1)
            level += jnp.dot(around, band, preferred_element_type=jnp.float32)
        inverse = 1.0 / (level * (1.0 / (2 * SMOOTH + 1)) + EPSILON)
        gath[p, win] = (psum[p] * jnp.concatenate([inverse, inverse], axis=1)).astype(jnp.bfloat16)

    def hand_on(p, source, way):
        item = gath.at[p, source]
        return remote(item, item, g_send.at[p, source, way], g_recv.at[p, source], (sta, win + 1 - 2 * way))

    def serve(p, source):
        for i in range(2):
            w2 = jnp.where(win == 0, 2 + i, i)
            octet = gath.at[p, source, pl.ds(pl.multiple_of(w2 * 32, 32), 32)]
            remote(octet, part.at[p, 1, source], c_send.at[p], c_recv.at[p], ((sta + 2) % STA, w2)).start()

    def begin(p):
        @pl.when(win < WIN - 1)
        def _():
            hand_on(p, win, 0).start()

        @pl.when(win > 0)
        def _():
            hand_on(p, win, 1).start()

        @pl.when((win == 0) | (win == WIN - 1))
        def _():
            serve(p, win)

    def relay(p, d):
        for way in range(2):
            source = win - d if way == 0 else win + d

            @pl.when((source >= 0) & (source < WIN))
            def _(source=source, way=way):
                item = gath.at[p, source]
                pltpu.make_async_copy(item, item, g_recv.at[p, source]).wait()
                last = win == (WIN - 1 if way == 0 else 0)

                @pl.when(jnp.logical_not(last))
                def _():
                    hand_on(p, source, way).start()

                @pl.when(last)
                def _():
                    serve(p, source)

    def swap(p):
        @pl.when(core == 0)
        def _():
            octet = gath.at[p, :, pl.ds(pl.multiple_of(win * 32, 32), 32)]
            remote(octet, part.at[p, 0], x_send.at[p], x_recv.at[p], other_core).start()

        @pl.when(core == 1)
        def _():
            pltpu.make_async_copy(part.at[p, 1], part.at[p, 1], c_recv.at[p]).wait()
            remote(part.at[p, 1], part.at[p, 0], x_send.at[p], x_recv.at[p], other_core).start()

    def finish(p, first):
        @pl.when(core == 0)
        def _():
            pltpu.make_async_copy(part.at[p, 1], part.at[p, 1], c_recv.at[p]).wait()

        pltpu.make_async_copy(part.at[p, 0], part.at[p, 0], x_recv.at[p]).wait()
        part32[...] = part[p].astype(jnp.float32)

        @pl.loop(0, PB // LANES)
        def _(t):
            re = pl.ds(pl.multiple_of(t * LANES, LANES), LANES)
            im = pl.ds(pl.multiple_of(PB + t * LANES, LANES), LANES)
            for g in range(4):
                r = g // 2
                sums = [[[jnp.zeros((8, LANES), jnp.float32) for _ in range(2)] for _ in range(4)] for _ in range(4)]
                for w2 in range(WIN):
                    for pair in range(2):
                        own = []
                        for octet in range(4):
                            at = pl.ds(octet * 32 + pair * 16, 16)
                            own.append(
                                (gath[p, w2, at, re].astype(jnp.float32), gath[p, w2, at, im].astype(jnp.float32))
                            )
                        for e in range(2):
                            for jj in range(4):
                                row = (pair * 2 + e) * 8 + (g % 2) * 4 + jj
                                pr = jnp.broadcast_to(part32[r, w2, row : row + 1, re], (8, LANES))
                                pi = jnp.broadcast_to(part32[r, w2, row : row + 1, im], (8, LANES))
                                for octet in range(4):
                                    a = own[octet][0][e * 8 : e * 8 + 8]
                                    c = own[octet][1][e * 8 : e * 8 + 8]
                                    both = sums[jj][octet]
                                    both[0] = both[0] + pr * a + pi * c
                                    both[1] = both[1] + pr * c - pi * a
                for jj in range(4):
                    at = pl.ds((r * 8 + (g % 2) * 4 + jj) * 32, 32)
                    for half, lanes in enumerate((re, im)):
                        tile = jnp.concatenate([sums[jj][octet][half] for octet in range(4)], axis=0)
                        stack[at, lanes] = tile.astype(jnp.bfloat16)

        @pl.loop(0, LAGS // 512)
        def _(n):
            lanes = pl.ds(pl.multiple_of(n * 512, 512), 512)
            more = jnp.dot(stack[...], table[p, :, lanes], preferred_element_type=jnp.float32)
            if first:
                acc[:, lanes] = more
            else:
                acc[:, lanes] += more

    order = (1, 2, 3, 0)
    for p in range(3):
        magnitude(p)
    for t in range(PIECES + 4):
        if t < PIECES:
            if t == 1:
                magnitude(3)
            whiten(order[t])
            begin(order[t])
        for d in range(1, WIN):
            if 0 <= t - d < PIECES:
                relay(order[t - d], d)
        if t >= 4:
            finish(order[t - 4], t == 4)
        if 0 <= t - 3 < PIECES:
            swap(order[t - 3])
    out[...] = acc[...].astype(jnp.bfloat16).reshape(out.shape)

    def gone(like, semaphore):
        pltpu.make_async_copy(like, like, semaphore).wait()

    gone(tag_s.at[pl.ds(0, 3)], t_send.at[0])
    gone(table.at[0, pl.ds(0, 112), pl.ds(0, 512)], t_send.at[1])
    for p in range(PIECES):
        gone(sbuf.at[p, pl.ds(0, 3)], a_send.at[p])
        gone(table.at[p, pl.ds(0, 112)], b_send.at[p])
        gone(zsend.at[p], z_send.at[p])
        gone(part.at[p, 0], x_send.at[p])

        @pl.when((win == 0) | (win == WIN - 1))
        def _():
            gone(part.at[p], c_send.at[p])

        for d in range(WIN):
            for way in range(2):
                source = win - d if way == 0 else win + d
                more = (source >= 0) & (source < WIN) & (win != (WIN - 1 if way == 0 else 0))

                @pl.when(more)
                def _(source=source, way=way):
                    gone(gath.at[p, source], g_send.at[p, source, way])


def angles(multiples):
    turns = np.outer(multiples, np.arange(LAGS) - LAGS // 2) % (4 * BINS)
    return turns * (2.0 * math.pi / (4 * BINS))


def shards(records, record_block, record_station, quality):
    hours, count, wide = records.shape
    scaling = 1.0 / math.sqrt(2.0 * BINS * hours * WIN)
    coarse, fine = angles(np.arange(BINS // 32) * 32 + 1), angles(np.arange(32))
    cos_u, sin_u = jnp.asarray(np.cos(coarse) * scaling, jnp.float32), jnp.asarray(np.sin(coarse) * scaling, jnp.float32)
    cos_v, sin_v = jnp.asarray(np.cos(fine), jnp.float32), jnp.asarray(np.sin(fine), jnp.float32)
    vmem = pl.BlockSpec(memory_space=pltpu.VMEM)
    dma = pltpu.SemaphoreType.DMA
    bf16, f32 = jnp.bfloat16, jnp.float32
    return pl.pallas_call(
        kernel,
        out_shape=jax.ShapeDtypeStruct((ROUNDS, 8, 32, LAGS), bf16),
        in_specs=[vmem] * 8,
        out_specs=vmem,
        scratch_shapes=[
            pltpu.VMEM((PIECES, 4, 4, 2, 16, PW), bf16),
            pltpu.VMEM((PIECES, 4, 4, 2, 16, PW), bf16),
            pltpu.VMEM((PIECES, 4, 4, 2, 16, PW), bf16),
            pltpu.VMEM((4, 4, 2, 16, LANES), bf16),
            pltpu.VMEM((4, 4, 2, 16, LANES), bf16),
            pltpu.VMEM((4, 4, 2, 16, LANES), bf16),
            pltpu.VMEM((256, PLANE * 16), bf16),
            pltpu.VMEM((PIECES, 128, PW), f32),
            pltpu.VMEM((PIECES, 128, PW), bf16),
            pltpu.VMEM((PIECES, 128, PW), bf16),
            pltpu.VMEM((PIECES, 128, PB), bf16),
            pltpu.VMEM((PIECES, 128, PB), bf16),
            pltpu.VMEM((PIECES, WIN, 128, PW), bf16),
            pltpu.VMEM((PIECES, ROUNDS, WIN, 32, PW), bf16),
            pltpu.VMEM((ROUNDS, WIN, 32, PW), f32),
            pltpu.VMEM((PIECES, PW, LAGS), bf16),
            pltpu.VMEM((512, PW), bf16),
            pltpu.VMEM((512, LAGS), f32),
            dma((PIECES,)), dma((PIECES,)), dma((PIECES,)), dma((PIECES,)), dma((2,)), dma((2,)),
            dma((PIECES,)), dma((PIECES,)), dma((PIECES, WIN, 2)), dma((PIECES, WIN)),
            dma((PIECES,)), dma((PIECES,)), dma((PIECES,)), dma((PIECES,)),
        ],
        compiler_params=pltpu.CompilerParams(
            collective_id=0, has_side_effects=True, vmem_limit_bytes=56 * 2**20
        ),
        name="correlate",
    )(record_block.reshape(hours, 1, count), record_station, quality, records.reshape(hours * count, wide), cos_u, sin_u, cos_v, sin_v)


def solution(mesh):
    in_specs = (P("win", "sta", None), P("win", "sta", None), P("win", "sta"), P("win", "sta"))
    out_specs = P(None, "win", "sta", None)
    return jax.shard_map(shards, mesh=mesh, in_specs=in_specs, out_specs=out_specs, check_vma=False)
```

time: 137 us -> 113 us (0.82)
  Pallas kernels: 128 us -> 110 us
  local copies, waits for them, and re-layouts: 6.75 us -> 3.16 us
  other arithmetic: 1.95 us -> 0 us
    pallas_call x1, Pallas kernels: 128 us -> 110 us  [shards(): pl.pallas_call(kernel, out_shape=jax.ShapeDtypeStruct((ROUNDS, 8, 32, LAG...]
    another operation x3 -> x0, local copies, waits for them, and re-layouts: 1.61 us -> none  [shards(): jnp.stack([a.reshape(hours * count) for a in (record_block, record_statio...]
    reshape x1 -> x0, local copies, waits for them, and re-layouts: 1.48 us -> none  [shards(): record_block.reshape(hours * count, 1)]
    unnamed x2 -> x1, local copies, waits for them, and re-layouts: 3.67 us -> 3.16 us
where the time goes in v1:
time: 113 us
  Pallas kernels  110 us (97%)
  local copies, waits for them, and re-layouts  3.16 us (3%)
    pallas_call x1, Pallas kernels, shards(): pl.pallas_call(kernel, out_shape=jax.ShapeDtypeStruct((ROUNDS, 8, 32, LAG...  110 us
    unnamed x1, local copies, waits for them, and re-layouts  3.16 us

profile of v1, /device:TPU:1, one launch (start us, length us, event | category | flops | bytes accessed | tf_op | source)
XLA Modules:
  0.0 113.2 jit_solution(964345256046422757)
XLA Ops:
  0.0 110.0 %correlate.1 = bf16[2,8,32,2048]{3,2,1,0:T(8,128)(2,1)} custom-call(s32[4,1,64]{2,1,0:T(1,128)} %bitcast.3, s32[4,64]{1,0:T(4,128)} %stations.1, s32[4,64]{1,0:T(4,128)} %quality.1, bf16[256,2048]{1,0:T(8,128)(2,1)} %bitcast.2, f32[32,2048]{1,0:T(8,128)} %constant.8.clone.cos_u, f32[32,2048]{1,0:T(8,128)} %constant.9.clone.sin_u, ...), custom_call_target="tpu_custom_call" | custom-call | tf_op jit(solution)/shard_map/correlate/pallas_call | solution.py:327
  110.0 3.2 %copy.10 = bf16[2,8,32,2048]{3,2,1,0:T(8,128)(2,1)} copy(bf16[2,8,32,2048]{3,2,1,0:T(8,128)(2,1)} %correlate.1) | data formatting | bytes 4194304

commit v2 on v1

--- a/solution.py
+++ b/solution.py
@@ -24,6 +24,15 @@
 PW = 2 * PB
 LANES = 128
 
+OFFSETS = [(0, 0, 1)] + [
+    (dy, dx, dc)
+    for dy, dx in (
+        (0, 1), (1, 0), (0, 3), (3, 0), (2, 2), (1, 1), (3, 3), (1, 3), (3, 1), (0, 2), (2, 0), (1, 2), (2, 1), (3, 2), (2, 3)
+    )
+    for dc in range(2)
+]
+
+
 def remote(src, dst, send, recv, device):
     return pltpu.make_async_remote_copy(
         src_ref=src, dst_ref=dst, send_sem=send, recv_sem=recv, device_id=device, device_id_type=MESH
@@ -32,22 +41,23 @@
 
 def kernel(
     blocks, stations, quality, rec, cos_u, sin_u, cos_v, sin_v, out,
-    sbuf, xbuf, rbuf, tag_s, tag_x, tag_r, assign, psum, zsend, zrecv, mag_hi, mag_lo, gath, part, part32, table, stack, acc,
-    a_send, a_recv, b_send, b_recv, t_send, t_recv, z_send, z_recv, g_send, g_recv, c_send, c_recv, x_send, x_recv,
+    sbuf, rbuf, tag_s, tag_r, assign, psum, zsend, zrecv, mag_hi, mag_lo, gath, part, part32, table, stack, acc,
+    b_send, b_recv, t_send, t_recv, z_send, z_recv, g_send, g_recv, c_send, c_recv, x_send, x_recv,
 ):
     sta, win = lax.axis_index("sta"), lax.axis_index("win")
     y, x, zh, core = sta // 16, (sta // 4) % 4, (sta // 2) % 2, sta % 2
 
-    def in_plane(y2, x2, c2):
-        return (((y2 * 4 + x2) * 2 + zh) * 2 + c2, win)
+    slot = (sta // 4) * 2 + core
+
+    def plane_peer(offset):
+        y2, x2, c2 = (y + offset[0]) % 4, (x + offset[1]) % 4, (core + offset[2]) % 2
+        return (((y2 * 4 + x2) * 2 + zh) * 2 + c2, win), (y2 * 4 + x2) * 2 + c2
 
     z_peer = (sta + 2 - 4 * zh, win)
     other_core = (sta + 1 - 2 * core, win)
 
     barrier = pltpu.get_barrier_semaphore()
-    greeted = [z_peer, other_core] + [(sta, (win + d) % WIN) for d in range(1, WIN)]
-    greeted += [in_plane((y + d) % 4, x, (core + dc) % 2) for d in range(1, 4) for dc in range(2)]
-    greeted += [in_plane(y, (x + d) % 4, (core + dc) % 2) for d in range(1, 4) for dc in range(2)]
+    greeted = [plane_peer(o)[0] for o in OFFSETS] + [z_peer] + [(sta, (win + d) % WIN) for d in range(1, WIN)]
     greeted += [((sta + d) % STA, w2) for d in (2, STA - 2) for w2 in range(WIN)]
     for device in greeted:
         pl.semaphore_signal(barrier, inc=1, device_id=device, device_id_type=MESH)
@@ -72,41 +82,19 @@
 
     pl.semaphore_wait(barrier, len(greeted))
 
-    def spread(source, between, send, recv, x_first):
-        for d in range(1, 4):
-            if x_first:
-                x2 = (x + d) % 4
-                remote(source.at[:, x2], between.at[x], send, recv, in_plane(y, x2, core)).start()
-            else:
-                y2 = (y + d) % 4
-                remote(source.at[y2], between.at[y], send, recv, in_plane(y2, x, core)).start()
-        own = source.at[:, x] if x_first else source.at[y]
-        pltpu.make_async_copy(own, between.at[x if x_first else y], recv).start()
-
-    def deliver(between, arrived, recv, send_on, recv_on, x_first):
-        pltpu.make_async_copy(between, between, recv).wait()
-        for d in (1, 2, 3, 0):
-            for dc in (1, 0):
-                c2 = (core + dc) % 2
-                if x_first:
-                    y2 = (y + d) % 4
-                    src, dst, device = between.at[:, y2, c2], arrived.at[y, :, core], in_plane(y2, x, c2)
-                else:
-                    x2 = (x + d) % 4
-                    src, dst, device = between.at[:, x2, c2], arrived.at[:, x, core], in_plane(y, x2, c2)
-                if d or dc:
-                    remote(src, dst, send_on, recv_on, device).start()
-                else:
-                    pltpu.make_async_copy(src, dst, recv_on).start()
-
-    spread(tag_s, tag_x, t_send.at[0], t_recv.at[0], True)
+    def spread(source, arrived, send, recv):
+        for offset in OFFSETS:
+            device, place = plane_peer(offset)
+            remote(source.at[place], arrived.at[slot], send, recv, device).start()
+        pltpu.make_async_copy(source.at[slot], arrived.at[slot], recv).start()
+
+    spread(tag_s, tag_r, t_send, t_recv)
     for p in range(PIECES):
         for half in range(2):
             lanes = pl.ds(half * BINS + p * PB, PB)
             packed = jnp.dot(placing, rec[:, lanes], preferred_element_type=jnp.float32)
-            sbuf[p, :, :, :, :, half * PB : (half + 1) * PB] = packed.astype(jnp.bfloat16).reshape(4, 4, 2, 16, PB)
-        spread(sbuf.at[p], xbuf.at[p], a_send.at[p], a_recv.at[p], p % 2 == 0)
-    deliver(tag_x, tag_r, t_recv.at[0], t_send.at[1], t_recv.at[1], True)
+            sbuf[p, :, :, half * PB : (half + 1) * PB] = packed.astype(jnp.bfloat16).reshape(PLANE, 16, PB)
+        spread(sbuf.at[p], rbuf.at[p], b_send.at[p], b_recv.at[p])
 
     def weigh(p):
         @pl.loop(0, PB // 32)
@@ -120,14 +108,10 @@
                 table[p, pl.ds(row, 32), lanes] = (cu * cv - su * sv).astype(jnp.bfloat16)
                 table[p, pl.ds(PB + row, 32), lanes] = (-(su * cv) - cu * sv).astype(jnp.bfloat16)
 
-    weigh(0)
-    weigh(1)
     for p in range(PIECES):
-        deliver(xbuf.at[p], rbuf.at[p], a_recv.at[p], b_send.at[p], b_recv.at[p], p % 2 == 0)
-    weigh(2)
-    weigh(3)
-
-    pltpu.make_async_copy(tag_r, tag_r, t_recv.at[1]).wait()
+        weigh(p)
+
+    pltpu.make_async_copy(tag_r, tag_r, t_recv).wait()
     label = tag_r[...].astype(jnp.float32).astype(jnp.int32).reshape(PLANE * 16, LANES) - 1
     row_id = lax.broadcasted_iota(jnp.int32, (PLANE * 16, LANES), 0)
     member = ((row_id // 2 + zh) % 2) * 128 + (label // 8) * 32 + ((row_id // 4) % 4) * 8 + label % 8
@@ -288,11 +272,9 @@
     def gone(like, semaphore):
         pltpu.make_async_copy(like, like, semaphore).wait()
 
-    gone(tag_s.at[pl.ds(0, 3)], t_send.at[0])
-    gone(table.at[0, pl.ds(0, 112), pl.ds(0, 512)], t_send.at[1])
+    gone(tag_s.at[pl.ds(0, PLANE - 1)], t_send)
     for p in range(PIECES):
-        gone(sbuf.at[p, pl.ds(0, 3)], a_send.at[p])
-        gone(table.at[p, pl.ds(0, 112)], b_send.at[p])
+        gone(sbuf.at[p, pl.ds(0, PLANE - 1)], b_send.at[p])
         gone(zsend.at[p], z_send.at[p])
         gone(part.at[p, 0], x_send.at[p])
 
@@ -330,12 +312,10 @@
         in_specs=[vmem] * 8,
         out_specs=vmem,
         scratch_shapes=[
-            pltpu.VMEM((PIECES, 4, 4, 2, 16, PW), bf16),
-            pltpu.VMEM((PIECES, 4, 4, 2, 16, PW), bf16),
-            pltpu.VMEM((PIECES, 4, 4, 2, 16, PW), bf16),
-            pltpu.VMEM((4, 4, 2, 16, LANES), bf16),
-            pltpu.VMEM((4, 4, 2, 16, LANES), bf16),
-            pltpu.VMEM((4, 4, 2, 16, LANES), bf16),
+            pltpu.VMEM((PIECES, PLANE, 16, PW), bf16),
+            pltpu.VMEM((PIECES, PLANE, 16, PW), bf16),
+            pltpu.VMEM((PLANE, 16, LANES), bf16),
+            pltpu.VMEM((PLANE, 16, LANES), bf16),
             pltpu.VMEM((256, PLANE * 16), bf16),
             pltpu.VMEM((PIECES, 128, PW), f32),
             pltpu.VMEM((PIECES, 128, PW), bf16),
@@ -348,7 +328,7 @@
             pltpu.VMEM((PIECES, PW, LAGS), bf16),
             pltpu.VMEM((512, PW), bf16),
             pltpu.VMEM((512, LAGS), f32),
-            dma((PIECES,)), dma((PIECES,)), dma((PIECES,)), dma((PIECES,)), dma((2,)), dma((2,)),
+            dma((PIECES,)), dma((PIECES,)), dma, dma,
             dma((PIECES,)), dma((PIECES,)), dma((PIECES, WIN, 2)), dma((PIECES, WIN)),
             dma((PIECES,)), dma((PIECES,)), dma((PIECES,)), dma((PIECES,)),
         ],

time: 113 us -> 103 us (0.912)
  Pallas kernels: 110 us -> 100 us
    pallas_call x1, Pallas kernels: 110 us -> 100 us  [shards(): pl.pallas_call(kernel, out_shape=jax.ShapeDtypeStruct((ROUNDS, 8, 32, LAG...]
where the time goes in v2:
time: 103 us
  Pallas kernels  100 us (97%)
  local copies, waits for them, and re-layouts  3.16 us (3%)
    pallas_call x1, Pallas kernels, shards(): pl.pallas_call(kernel, out_shape=jax.ShapeDtypeStruct((ROUNDS, 8, 32, LAG...  100 us
    unnamed x1, local copies, waits for them, and re-layouts  3.16 us

profile of v2, /device:TPU:1, one launch (start us, length us, event | category | flops | bytes accessed | tf_op | source)
XLA Modules:
  0.0 103.3 jit_solution(15876222925031864345)
XLA Ops:
  0.0 100.2 %correlate.1 = bf16[2,8,32,2048]{3,2,1,0:T(8,128)(2,1)} custom-call(s32[4,1,64]{2,1,0:T(1,128)} %bitcast.3, s32[4,64]{1,0:T(4,128)} %stations.1, s32[4,64]{1,0:T(4,128)} %quality.1, bf16[256,2048]{1,0:T(8,128)(2,1)} %bitcast.2, f32[32,2048]{1,0:T(8,128)} %constant.8.clone.cos_u, f32[32,2048]{1,0:T(8,128)} %constant.9.clone.sin_u, ...), custom_call_target="tpu_custom_call" | custom-call | tf_op jit(solution)/shard_map/correlate/pallas_call | solution.py:309
  100.2 3.2 %copy.10 = bf16[2,8,32,2048]{3,2,1,0:T(8,128)(2,1)} copy(bf16[2,8,32,2048]{3,2,1,0:T(8,128)(2,1)} %correlate.1) | data formatting | bytes 4194304

commit v3 on v2

--- a/solution.py
+++ b/solution.py
@@ -191,12 +191,13 @@
                 def _():
                     serve(p, source)
 
-    def swap(p):
+    def swap_own(p):
         @pl.when(core == 0)
         def _():
             octet = gath.at[p, :, pl.ds(pl.multiple_of(win * 32, 32), 32)]
             remote(octet, part.at[p, 0], x_send.at[p], x_recv.at[p], other_core).start()
 
+    def swap(p):
         @pl.when(core == 1)
         def _():
             pltpu.make_async_copy(part.at[p, 1], part.at[p, 1], c_recv.at[p]).wait()
@@ -216,30 +217,32 @@
             im = pl.ds(pl.multiple_of(PB + t * LANES, LANES), LANES)
             for g in range(4):
                 r = g // 2
-                sums = [[[jnp.zeros((8, LANES), jnp.float32) for _ in range(2)] for _ in range(4)] for _ in range(4)]
+                sums = [[[jnp.zeros((8, LANES), jnp.float32) for _ in range(3)] for _ in range(4)] for _ in range(4)]
                 for w2 in range(WIN):
                     for pair in range(2):
                         own = []
                         for octet in range(4):
                             at = pl.ds(octet * 32 + pair * 16, 16)
-                            own.append(
-                                (gath[p, w2, at, re].astype(jnp.float32), gath[p, w2, at, im].astype(jnp.float32))
-                            )
+                            a, c = gath[p, w2, at, re].astype(jnp.float32), gath[p, w2, at, im].astype(jnp.float32)
+                            own.append((a, c, a + c))
                         for e in range(2):
                             for jj in range(4):
                                 row = (pair * 2 + e) * 8 + (g % 2) * 4 + jj
                                 pr = jnp.broadcast_to(part32[r, w2, row : row + 1, re], (8, LANES))
                                 pi = jnp.broadcast_to(part32[r, w2, row : row + 1, im], (8, LANES))
+                                pd = pr - pi
                                 for octet in range(4):
-                                    a = own[octet][0][e * 8 : e * 8 + 8]
-                                    c = own[octet][1][e * 8 : e * 8 + 8]
-                                    both = sums[jj][octet]
-                                    both[0] = both[0] + pr * a + pi * c
-                                    both[1] = both[1] + pr * c - pi * a
+                                    a, c, ac = (v[e * 8 : e * 8 + 8] for v in own[octet])
+                                    three = sums[jj][octet]
+                                    three[0] = three[0] + pr * a
+                                    three[1] = three[1] + pi * c
+                                    three[2] = three[2] + pd * ac
                 for jj in range(4):
                     at = pl.ds((r * 8 + (g % 2) * 4 + jj) * 32, 32)
                     for half, lanes in enumerate((re, im)):
-                        tile = jnp.concatenate([sums[jj][octet][half] for octet in range(4)], axis=0)
+                        tile = jnp.concatenate(
+                            [s[2] - s[0] + s[1] if half else s[0] + s[1] for s in sums[jj]], axis=0
+                        )
                         stack[at, lanes] = tile.astype(jnp.bfloat16)
 
         @pl.loop(0, LAGS // 512)
@@ -260,9 +263,11 @@
                 magnitude(3)
             whiten(order[t])
             begin(order[t])
-        for d in range(1, WIN):
+        for d in (3, 2, 1):
             if 0 <= t - d < PIECES:
                 relay(order[t - d], d)
+                if d == 3:
+                    swap_own(order[t - d])
         if t >= 4:
             finish(order[t - 4], t == 4)
         if 0 <= t - 3 < PIECES:
@@ -290,6 +295,19 @@
                 @pl.when(more)
                 def _(source=source, way=way):
                     gone(gath.at[p, source], g_send.at[p, source, way])
+
+
+def hand_over(src, dst, held, came, left):
+    places = [(r, pl.ds(j, 2)) for r in range(ROUNDS) for j in range(0, 8, 2)]
+    into = [pltpu.make_async_copy(src.at[at], held.at[at], came.at[i]) for i, at in enumerate(places)]
+    onto = [pltpu.make_async_copy(held.at[at], dst.at[at], left.at[i]) for i, at in enumerate(places)]
+    for copy in into:
+        copy.start()
+    for before, after in zip(into, onto):
+        before.wait()
+        after.start()
+    for copy in onto:
+        copy.wait()
 
 
 def angles(multiples):
@@ -306,7 +324,7 @@
     vmem = pl.BlockSpec(memory_space=pltpu.VMEM)
     dma = pltpu.SemaphoreType.DMA
     bf16, f32 = jnp.bfloat16, jnp.float32
-    return pl.pallas_call(
+    result = pl.pallas_call(
         kernel,
         out_shape=jax.ShapeDtypeStruct((ROUNDS, 8, 32, LAGS), bf16),
         in_specs=[vmem] * 8,
@@ -337,6 +355,15 @@
         ),
         name="correlate",
     )(record_block.reshape(hours, 1, count), record_station, quality, records.reshape(hours * count, wide), cos_u, sin_u, cos_v, sin_v)
+    anywhere = pl.BlockSpec(memory_space=pl.ANY)
+    return pl.pallas_call(
+        hand_over,
+        out_shape=jax.ShapeDtypeStruct(result.shape, result.dtype),
+        in_specs=[anywhere],
+        out_specs=anywhere,
+        scratch_shapes=[pltpu.VMEM(result.shape, bf16), dma((8,)), dma((8,))],
+        name="hand_over",
+    )(result)
 
 
 def solution(mesh):

time: 103 us -> 99.6 us (0.967); the launches traced: 103 us -> 98.2 us
  local copies, waits for them, and re-layouts: 3.16 us -> 0 us
  Pallas kernels: 100 us -> 98.2 us
    pallas_call x1, Pallas kernels: 100 us -> 95.8 us  [shards(): pl.pallas_call(kernel, out_shape=jax.ShapeDtypeStruct((ROUNDS, 8, 32, LAG...]
    unnamed x1 -> x0, local copies, waits for them, and re-layouts: 3.16 us -> none
    pallas_call x0 -> x1, Pallas kernels: none -> 2.39 us  [shards(): pl.pallas_call(hand_over, out_shape=jax.ShapeDtypeStruct(result.shape, re...]
where the time goes in v3:
time: 99.6 us; the launch traced here: 98.2 us
  Pallas kernels  98.2 us (99%)
    pallas_call x1, Pallas kernels, shards(): pl.pallas_call(kernel, out_shape=jax.ShapeDtypeStruct((ROUNDS, 8, 32, LAG...  95.8 us
    pallas_call x1, Pallas kernels, shards(): pl.pallas_call(hand_over, out_shape=jax.ShapeDtypeStruct(result.shape, re...  2.39 us

profile of v3, /device:TPU:1, one launch (start us, length us, event | category | flops | bytes accessed | tf_op | source)
XLA Modules:
  0.0 98.2 jit_solution(2529710354890241394)
XLA Ops:
  0.0 95.8 %correlate.1.src = bf16[2,8,32,2048]{3,2,1,0:T(8,128)(2,1)} custom-call(s32[4,1,64]{2,1,0:T(1,128)} %bitcast.3, s32[4,64]{1,0:T(4,128)} %stations.1, s32[4,64]{1,0:T(4,128)} %quality.1, bf16[256,2048]{1,0:T(8,128)(2,1)} %bitcast.2, f32[32,2048]{1,0:T(8,128)} %constant.8.clone.cos_u, f32[32,2048]{1,0:T(8,128)} %constant.9.clone.sin_u, ...), custom_call_target="tpu_custom_call" | custom-call | tf_op jit(solution)/shard_map/correlate/pallas_call | solution.py:327
  95.8 2.4 %hand_over.1 = bf16[2,8,32,2048]{3,2,1,0:T(8,128)(2,1)} custom-call(bf16[2,8,32,2048]{3,2,1,0:T(8,128)(2,1)} %correlate.1.src), custom_call_target="tpu_custom_call" | custom-call | tf_op jit(solution)/shard_map/hand_over/pallas_call | solution.py:359

commit v4 on v3

--- a/solution.py
+++ b/solution.py
@@ -203,7 +203,7 @@
             pltpu.make_async_copy(part.at[p, 1], part.at[p, 1], c_recv.at[p]).wait()
             remote(part.at[p, 1], part.at[p, 0], x_send.at[p], x_recv.at[p], other_core).start()
 
-    def finish(p, first):
+    def finish(p, first, last):
         @pl.when(core == 0)
         def _():
             pltpu.make_async_copy(part.at[p, 1], part.at[p, 1], c_recv.at[p]).wait()
@@ -249,7 +249,9 @@
         def _(n):
             lanes = pl.ds(pl.multiple_of(n * 512, 512), 512)
             more = jnp.dot(stack[...], table[p, :, lanes], preferred_element_type=jnp.float32)
-            if first:
+            if last:
+                out[:, :, :, lanes] = (acc[:, lanes] + more).astype(jnp.bfloat16).reshape(ROUNDS, 8, 32, 512)
+            elif first:
                 acc[:, lanes] = more
             else:
                 acc[:, lanes] += more
@@ -269,10 +271,9 @@
                 if d == 3:
                     swap_own(order[t - d])
         if t >= 4:
-            finish(order[t - 4], t == 4)
+            finish(order[t - 4], t == 4, t == PIECES + 3)
         if 0 <= t - 3 < PIECES:
             swap(order[t - 3])
-    out[...] = acc[...].astype(jnp.bfloat16).reshape(out.shape)
 
     def gone(like, semaphore):
         pltpu.make_async_copy(like, like, semaphore).wait()

time: 99.6 us -> 99.4 us (level)
  no operation moved by 1% of the time
where the time goes in v4:
time: 99.4 us; the launch traced here: 98 us
  Pallas kernels  98 us (99%)
    pallas_call x1, Pallas kernels, shards(): pl.pallas_call(kernel, out_shape=jax.ShapeDtypeStruct((ROUNDS, 8, 32, LAG...  95.6 us
    pallas_call x1, Pallas kernels, shards(): pl.pallas_call(hand_over, out_shape=jax.ShapeDtypeStruct(result.shape, re...  2.39 us

profile of v4, /device:TPU:1, one launch (start us, length us, event | category | flops | bytes accessed | tf_op | source)
XLA Modules:
  0.0 98.0 jit_solution(13379880884677601139)
XLA Ops:
  0.0 95.6 %correlate.1.src = bf16[2,8,32,2048]{3,2,1,0:T(8,128)(2,1)} custom-call(s32[4,1,64]{2,1,0:T(1,128)} %bitcast.3, s32[4,64]{1,0:T(4,128)} %stations.1, s32[4,64]{1,0:T(4,128)} %quality.1, bf16[256,2048]{1,0:T(8,128)(2,1)} %bitcast.2, f32[32,2048]{1,0:T(8,128)} %constant.8.clone.cos_u, f32[32,2048]{1,0:T(8,128)} %constant.9.clone.sin_u, ...), custom_call_target="tpu_custom_call" | custom-call | tf_op jit(solution)/shard_map/correlate/pallas_call | solution.py:328
  95.6 2.4 %hand_over.1 = bf16[2,8,32,2048]{3,2,1,0:T(8,128)(2,1)} custom-call(bf16[2,8,32,2048]{3,2,1,0:T(8,128)(2,1)} %correlate.1.src), custom_call_target="tpu_custom_call" | custom-call | tf_op jit(solution)/shard_map/hand_over/pallas_call | solution.py:360
